TPU v7x, 128 devices: a whole 4x4x4 slice. The times are simulated.
128 devices in a mesh: dp: 32 (over x, z, y_hi), seq: 4 (over y_lo, core).
Axes of the slice: x: 4, y: 4 (y_hi: 2, y_lo: 2; y = y_hi * 2 + y_lo), z: 4, core: 2. Of those that a mesh axis runs over, the one named last changes fastest.
Arguments:
- key_tokens: bfloat16 [32, 1024, 2048], P('dp', 'seq'), may hold values from -4 to 4
- value_tokens: bfloat16 [32, 1024, 2048], P('dp', 'seq'), may hold values from -6 to 6
- query_tokens: bfloat16 [32, 1024, 2048], P('dp', 'seq'), may hold values from -6 to 6
- cotangent: bfloat16 [32, 1024, 2048], P('dp', 'seq'), may hold values from -0.03125 to 0.03125
- base_weight: bfloat16 [2048, 2048], P('dp'), may hold values from -0.125 to 0.125
- factors: float32 [2, 2048, 128], replicated, may hold values from -0.375 to 0.375
Outputs:
- recalled: bfloat16 [32, 1024, 2048], P('dp', 'seq')
- base_grad: float32 [2048, 2048], P('dp')
All inputs are finite; a program needn't handle non-finite values.
Results may differ from a plain program's by a relative error of at most 0.0012.
Values may be sent and summed in bfloat16 or wider, within the bound.
No kernel may reach another device: no remote copies, remote signals or barrier semaphores. Data moves between devices by JAX's collectives and lax.ppermute only.
A program may use at most 128 MiB of HBM per device.

v0:
```python
import jax
import jax.numpy as jnp
from jax import lax
from jax.sharding import PartitionSpec as P

GROUP = 256


learn_rate = 0.01
highest = lax.Precision.HIGHEST


def passed_along(value, axis, by):
    devices = lax.axis_size(axis)
    pairs = [(i, i + by) for i in range(devices) if 0 <= i + by < devices]
    return lax.ppermute(value, axis, pairs)


def memory_step(memory, group_keys, group_values, group_queries, group_proj):
    left_factor = memory[:, 0]
    right_factor = memory[:, 1]
    key_left = jnp.einsum("btd,bdr->btr", group_keys, left_factor, precision=highest)
    query_left = jnp.einsum("btd,bdr->btr", group_queries, left_factor, precision=highest)
    lowrank = jnp.einsum("btr,bdr->btd", query_left, right_factor, precision=highest)
    residue = (
        group_proj
        + jnp.einsum("btr,bdr->btd", key_left, right_factor, precision=highest)
        - group_values
    )
    residue_right = jnp.einsum("btd,bdr->btr", residue, right_factor, precision=highest)
    step_left = jnp.einsum("btd,btr->bdr", group_keys, residue_right, precision=highest) / GROUP
    step_right = jnp.einsum("btd,btr->bdr", residue, key_left, precision=highest) / GROUP
    updated = jnp.stack(
        [left_factor - learn_rate * step_left, right_factor - learn_rate * step_right], axis=1
    )
    return (updated, lowrank)


def per_device(key_tokens, value_tokens, query_tokens, cotangent, base_weight, factors):
    docs_here, slice_len, width = key_tokens.shape
    token_count = docs_here * slice_len
    stacked_rows = jnp.concatenate(
        [key_tokens.reshape(token_count, width), query_tokens.reshape(token_count, width)], 0
    )
    columns = stacked_rows
    projected = jnp.dot(
        columns,
        lax.all_gather(base_weight, "dp", axis=0, tiled=True),
        preferred_element_type=jnp.float32,
    )
    key_proj = projected[:token_count].reshape(docs_here, slice_len, width)
    query_proj = projected[token_count:].reshape(docs_here, slice_len, width)
    key_wide = key_tokens.astype(jnp.float32)
    value_wide = value_tokens.astype(jnp.float32)
    query_wide = query_tokens.astype(jnp.float32)

    def local_chain(proj, memory):
        memory, lowrank = memory_step(memory, key_wide, value_wide, query_wide, proj)
        pieces = [lowrank]
        return (jnp.concatenate(pieces, 1), memory)

    initial = factors[None]
    seq_count = lax.axis_size("seq")
    position = lax.axis_index("seq")
    memory = initial
    for relay_step in range(seq_count - 1):
        _, passed = local_chain(key_proj, memory)
        moved = passed_along(passed, "seq", 1)
        memory = jnp.where(position == 0, initial, moved)
    (lowrank, final_memory), pullback = jax.vjp(local_chain, key_proj, memory)
    recalled = (query_proj + lowrank).astype(jnp.bfloat16)
    cot_wide = cotangent.astype(jnp.float32)
    memory_cot = jnp.zeros_like(final_memory)
    for relay_step in range(seq_count - 1):
        _, memory_grad = pullback((cot_wide, memory_cot))
        memory_cot = passed_along(memory_grad.astype(jnp.bfloat16), "seq", -1).astype(
            memory_grad.dtype
        )
    proj_grad, _ = pullback((cot_wide, memory_cot))
    grad_right = jnp.concatenate(
        [
            proj_grad.astype(jnp.bfloat16).reshape(token_count, width),
            cotangent.reshape(token_count, width),
        ],
        0,
    )
    columns = stacked_rows
    share = lax.psum_scatter(
        lax.dot_general(
            columns, grad_right, (((0,), (0,)), ((), ())), preferred_element_type=jnp.float32
        ),
        "dp",
        scatter_dimension=0,
        tiled=True,
    )
    base_grad = lax.psum(share, "seq")
    return (recalled, base_grad)


def solution(mesh):
    in_specs = (
        P("dp", "seq", None),
        P("dp", "seq", None),
        P("dp", "seq", None),
        P("dp", "seq", None),
        P("dp", None),
        P(),
    )
    out_specs = (P("dp", "seq", None), P("dp", None))
    return jax.shard_map(
        per_device, mesh=mesh, in_specs=in_specs, out_specs=out_specs, check_vma=False
    )
```

profile of v0, /device:TPU:1, one launch (start us, length us, event | category | flops | bytes accessed | tf_op | source)
XLA Modules:
  0.0 749.9 jit_solution(8047943990491671060)
XLA Ops:
  11.0 107.1 %all-gather.2.cloned.1.call-done = bf16[2048,2048]{1,0:T(8,128)(2,1)} async-done(((bf16[64,2048]{1,0:T(8,128)(2,1)}), bf16[2048,2048]{1,0:T(8,128)(2,1)}) %all-gather.2.cloned.1.call-update) | async-done | bytes 8388624 | tf_op jit(solution)/shard_map/all_gather | solution.py:48
  118.1 7.3 fusion.41
  132.9 3.4 collective-permute-start
  136.3 23.1 %collective-permute-done = f32[1,2,2048,128]{2,3,1,0:T(8,128)} collective-permute-done((f32[1,2,2048,128]{2,3,1,0:T(8,128)}, f32[1,2,2048,128]{2,3,1,0:T(8,128)}, u32[]{:S(2)}, u32[]{:S(2)}) %collective-permute-start) | collective-permute-done | bytes 2097184 | tf_op jit(solution)/shard_map/ppermute | solution.py:16
  162.8 2.1 fusion.10
  168.8 4.6 collective-permute-start.1
  173.5 22.7 %collective-permute-done.1 = f32[1,2,2048,128]{2,3,1,0:T(8,128)S(1)} collective-permute-done((f32[1,2,2048,128]{2,3,1,0:T(8,128)S(1)}, f32[1,2,2048,128]{2,3,1,0:T(8,128)S(1)}, u32[]{:S(2)}, u32[]{:S(2)}) %collective-permute-start.1) | collective-permute-done | bytes 2097184 | tf_op jit(solution)/shard_map/ppermute | solution.py:16
  203.8 5.0 collective-permute-start.2
  209.9 21.4 %collective-permute-done.2 = f32[1,2,2048,128]{2,3,1,0:T(8,128)S(1)} collective-permute-done((f32[1,2,2048,128]{2,3,1,0:T(8,128)S(1)}, f32[1,2,2048,128]{2,3,1,0:T(8,128)S(1)}, u32[]{:S(2)}, u32[]{:S(2)}) %collective-permute-start.2) | collective-permute-done | bytes 2097184 | tf_op jit(solution)/shard_map/ppermute | solution.py:16
  236.4 2.1 fusion.12
  243.6 2.4 fusion.43
  250.0 14.9 %collective-permute-done.3 = bf16[1,2,2048,128]{2,3,1,0:T(8,128)(2,1)S(1)} collective-permute-done((bf16[1,2,2048,128]{2,3,1,0:T(8,128)(2,1)S(1)}, bf16[1,2,2048,128]{2,3,1,0:T(8,128)(2,1)S(1)}, u32[]{:S(2)}, u32[]{:S(2)}) %collective-permute-start.3) | collective-permute-done | bytes 1048608 | tf_op jit(solution)/shard_map/ppermute | solution.py:16
  266.4 2.2 convolution_bitcast_fusion.20
  272.4 2.3 convolution_bitcast_fusion.13
  278.2 2.1 collective-permute-start.4
  280.3 14.0 %collective-permute-done.4 = bf16[1,2,2048,128]{2,3,1,0:T(8,128)(2,1)S(1)} collective-permute-done((bf16[1,2,2048,128]{2,3,1,0:T(8,128)(2,1)S(1)}, bf16[1,2,2048,128]{2,3,1,0:T(8,128)(2,1)S(1)}, u32[]{:S(2)}, u32[]{:S(2)}) %collective-permute-start.4) | collective-permute-done | bytes 1048608 | tf_op jit(solution)/shard_map/ppermute | solution.py:16
  295.7 2.2 convolution_bitcast_fusion.18
  301.8 2.3 convolution_bitcast_fusion.11
  307.6 2.2 collective-permute-start.5
  309.7 13.9 %collective-permute-done.5 = bf16[1,2,2048,128]{2,3,1,0:T(8,128)(2,1)S(1)} collective-permute-done((bf16[1,2,2048,128]{2,3,1,0:T(8,128)(2,1)S(1)}, bf16[1,2,2048,128]{2,3,1,0:T(8,128)(2,1)S(1)}, u32[]{:S(2)}, u32[]{:S(2)}) %collective-permute-start.5) | collective-permute-done | bytes 1048608 | tf_op jit(solution)/shard_map/ppermute | solution.py:16
  328.9 8.3 %fusion.37 = f32[2048,2048]{1,0:T(8,128)} fusion(bf16[256,2048]{1,0:T(8,128)(2,1)S(1)} %bitcast.413, bf16[256,2048]{1,0:T(8,128)(2,1)S(1)} %fusion.16, bf16[256,2048]{1,0:T(8,128)(2,1)S(1)} %bitcast.412, bf16[256,2048]{1,0:T(8,128)(2,1)S(1)} %bitcast.405), kind=kOutput, calls=%fused_computation.74 | convolution fusion | flops 4303355904 | bytes 20971520 | tf_op jit(solution)/shard_map/dot_general | solution.py:89
  337.2 359.6 %reduce-scatter.2.cloned.1.call-done = f32[64,2048]{1,0:T(8,128)} async-done(((f32[2048,2048]{1,0:T(8,128)}), f32[64,2048]{1,0:T(8,128)}) %reduce-scatter.2.cloned.1.call-update) | async-done | bytes 524304 | tf_op jit(solution)/shard_map/reduce_scatter | solution.py:88
  696.9 4.4 fusion.15
  701.3 39.8 %all-reduce.8.cloned.1.call-done = f32[64,2048]{1,0:T(8,128)} async-done(((f32[64,2048]{1,0:T(8,128)}), f32[64,2048]{1,0:T(8,128)}) %all-reduce.8.cloned.1.call-update) | async-done | bytes 524304 | tf_op jit(solution)/shard_map/psum | solution.py:96
  (79 shorter events, 65.8 us)
Async XLA Ops:
  7.2 110.9 %all-gather.2.cloned.1.call-start = ((), (), s32[]{:S(2)}) async-start(), calls=%async_computation.1 | async-start | bytes 8650752 | tf_op jit(solution)/shard_map/all_gather | solution.py:48
  7.9 2.1 copy-start
  7.9 688.9 %reduce-scatter.2.cloned.1.call-start = ((), (), s32[]{:S(2)}) async-start(), calls=%async_computation.2 | async-start | bytes 17301504 | tf_op jit(solution)/shard_map/reduce_scatter | solution.py:88
  10.0 186.2 %copy-start.1 = (f32[2,2048,128]{1,2,0:T(8,128)}, f32[2,2048,128]{1,2,0:T(8,128)S(1)}, u32[]{:S(2)}) copy-start(f32[2,2048,128]{1,2,0:T(8,128)S(1)} %copy.8) | copy-start | bytes 6291460
  118.1 7.3 copy-start.5
  125.4 2.0 copy-start.3
  132.9 26.5 %collective-permute-start = (f32[1,2,2048,128]{2,3,1,0:T(8,128)}, f32[1,2,2048,128]{2,3,1,0:T(8,128)}, u32[]{:S(2)}, u32[]{:S(2)}) collective-permute-start(f32[1,2,2048,128]{2,3,1,0:T(8,128)} %pad_maximum_fusion.1), channel_id=1, source_target_pairs={{0,1},{1,2},{2,3},{4,5},{5,6},{6,7},{8,9},{9,10},{10,11},{12,13},{... | collective-permute-start | bytes 6291464 | tf_op jit(solution)/shard_map/ppermute | solution.py:16
  159.3 3.2 copy-start.4
  161.3 1.4 copy-start.6
  168.8 27.4 %collective-permute-start.1 = (f32[1,2,2048,128]{2,3,1,0:T(8,128)S(1)}, f32[1,2,2048,128]{2,3,1,0:T(8,128)S(1)}, u32[]{:S(2)}, u32[]{:S(2)}) collective-permute-start(f32[1,2,2048,128]{2,3,1,0:T(8,128)S(1)} %pad_maximum_fusion.2), channel_id=1, source_target_pairs={{0,1},{1,2},{2,3},{4,5},{5,6},{6,7},{8,9},{9,10},{10,11},{12,13},{... | collective-permute-start | bytes 6291464 | tf_op jit(solution)/shard_map/ppermute | solution.py:16
  203.6 27.7 %copy-start.2 = (f32[2,2048,128]{1,2,0:T(8,128)S(1)}, f32[2,2048,128]{1,2,0:T(8,128)}, u32[]{:S(2)}) copy-start(f32[2,2048,128]{1,2,0:T(8,128)} %copy-done.1) | copy-start | bytes 6291460
  203.8 27.5 %collective-permute-start.2 = (f32[1,2,2048,128]{2,3,1,0:T(8,128)S(1)}, f32[1,2,2048,128]{2,3,1,0:T(8,128)S(1)}, u32[]{:S(2)}, u32[]{:S(2)}) collective-permute-start(f32[1,2,2048,128]{2,3,1,0:T(8,128)S(1)} %pad_maximum_fusion.3), channel_id=1, source_target_pairs={{0,1},{1,2},{2,3},{4,5},{5,6},{6,7},{8,9},{9,10},{10,11},{12,13},{... | collective-permute-start | bytes 6291464 | tf_op jit(solution)/shard_map/ppermute | solution.py:16
  209.9 21.6 %copy-start.7 = (bf16[1,256,2048]{2,1,0:T(8,128)(2,1)S(1)}, bf16[1,256,2048]{2,1,0:T(8,128)(2,1)}, u32[]{:S(2)}) copy-start(bf16[1,256,2048]{2,1,0:T(8,128)(2,1)} %param.8) | copy-start | bytes 3145732
  231.6 2.4 copy-start.8
  248.1 16.9 %collective-permute-start.3 = (bf16[1,2,2048,128]{2,3,1,0:T(8,128)(2,1)S(1)}, bf16[1,2,2048,128]{2,3,1,0:T(8,128)(2,1)S(1)}, u32[]{:S(2)}, u32[]{:S(2)}) collective-permute-start(bf16[1,2,2048,128]{2,3,1,0:T(8,128)(2,1)S(1)} %add_convert_fusion.2), channel_id=1, source_target_pairs={{1,0},{2,1},{3,2},{5,4},{6,5},{7,6},{9,8},{10,9},{11,10},{13,12},{... | collective-permute-start | bytes 3145736 | tf_op jit(solution)/shard_map/ppermute | solution.py:16
  278.2 16.1 %collective-permute-start.4 = (bf16[1,2,2048,128]{2,3,1,0:T(8,128)(2,1)S(1)}, bf16[1,2,2048,128]{2,3,1,0:T(8,128)(2,1)S(1)}, u32[]{:S(2)}, u32[]{:S(2)}) collective-permute-start(bf16[1,2,2048,128]{2,3,1,0:T(8,128)(2,1)S(1)} %add_convert_fusion.1), channel_id=1, source_target_pairs={{1,0},{2,1},{3,2},{5,4},{6,5},{7,6},{9,8},{10,9},{11,10},{13,12},{... | collective-permute-start | bytes 3145736 | tf_op jit(solution)/shard_map/ppermute | solution.py:16
  307.6 16.1 %collective-permute-start.5 = (bf16[1,2,2048,128]{2,3,1,0:T(8,128)(2,1)S(1)}, bf16[1,2,2048,128]{2,3,1,0:T(8,128)(2,1)S(1)}, u32[]{:S(2)}, u32[]{:S(2)}) collective-permute-start(bf16[1,2,2048,128]{2,3,1,0:T(8,128)(2,1)S(1)} %add_convert_fusion), channel_id=1, source_target_pairs={{1,0},{2,1},{3,2},{5,4},{6,5},{7,6},{9,8},{10,9},{11,10},{13,12},{... | collective-permute-start | bytes 3145736 | tf_op jit(solution)/shard_map/ppermute | solution.py:16
  337.2 403.9 %all-reduce.8.cloned.1.call-start = ((), (), s32[]{:S(2)}) async-start(), calls=%async_computation.3 | async-start | bytes 1048576 | tf_op jit(solution)/shard_map/psum | solution.py:96
Sparse Core Ops, SparseCore 0:
  11.0 107.0 all-gather.1
  337.3 359.5 reduce-scatter.1
  699.4 41.6 all-reduce.7
where the time goes:
time: 757 us; the launch traced here: 750 us
  waiting for transfers between devices  617 us (82%)
  matrix products  88.9 us (12%)
  starting transfers between devices  19.4 us (3%)
  between operations  14.8 us (2%)
    reduce_scatter x1, waiting for transfers between devices, per_device(): lax.psum_scatter(lax.dot_general(columns, grad_right, (((0,), (0,)), ((),...  360 us
    ppermute x6, waiting for transfers between devices, passed_along(): return lax.ppermute(value, axis, pairs)  110 us
    all_gather x1, waiting for transfers between devices, per_device(): lax.all_gather(base_weight, 'dp', axis=0, tiled=True)  107 us
    psum x1, waiting for transfers between devices, per_device(): base_grad = lax.psum(share, 'seq')  39.8 us
    ppermute x6, starting transfers between devices, passed_along(): return lax.ppermute(value, axis, pairs)  19.2 us
    dot_general x10, matrix products, memory_step(): jnp.einsum('btr,bdr->btd', key_left, right_factor, precision=highest)  19.1 us
    dot_general x10, matrix products, memory_step(): jnp.einsum('btd,bdr->btr', residue, right_factor, precision=highest)  17 us
    dot_general x9, matrix products, memory_step(): jnp.einsum('btd,btr->bdr', residue, key_left, precision=highest) / GROUP  16.1 us
  transfers between devices with their start and end apart: 9, of which 9 were waited for; matrix products, arithmetic and copies ran while one was open for 1% of the time, Pallas kernels for 0%

commit v1 on v0

v1 whole, which is shorter than its diff:
```python
import jax
import jax.numpy as jnp
from jax import lax
from jax.sharding import Mesh, PartitionSpec as P

GROUP = 256
DP = ("x", "z", "yh")
SEQ = ("yl", "c")
CHIPS = ("x", "z", "yh", "yl")

learn_rate = 0.01
highest = lax.Precision.HIGHEST


def swap_cores(value):
    return lax.ppermute(value, "c", [(0, 1), (1, 0)])


def memory_step(memory, group_keys, group_values, group_queries, group_proj):
    left_factor = memory[:, 0]
    right_factor = memory[:, 1]
    key_left = jnp.einsum("btd,bdr->btr", group_keys, left_factor, precision=highest)
    query_left = jnp.einsum("btd,bdr->btr", group_queries, left_factor, precision=highest)
    lowrank = jnp.einsum("btr,bdr->btd", query_left, right_factor, precision=highest)
    residue = (
        group_proj
        + jnp.einsum("btr,bdr->btd", key_left, right_factor, precision=highest)
        - group_values
    )
    residue_right = jnp.einsum("btd,bdr->btr", residue, right_factor, precision=highest)
    step_left = jnp.einsum("btd,btr->bdr", group_keys, residue_right, precision=highest) / GROUP
    step_right = jnp.einsum("btd,btr->bdr", residue, key_left, precision=highest) / GROUP
    updated = jnp.stack(
        [left_factor - learn_rate * step_left, right_factor - learn_rate * step_right], axis=1
    )
    return (updated, lowrank)


def per_device(key_tokens, value_tokens, query_tokens, cotangent, base_weight, factors):
    _, slice_len, width = key_tokens.shape
    half = width // 2
    core = lax.axis_index("c")
    position = lax.axis_index("yl") * 2 + core
    seq_count = 4

    def own_half(array):
        return lax.dynamic_slice_in_dim(array, core * half, half, 1)

    def other_half(array):
        return lax.dynamic_slice_in_dim(array, (1 - core) * half, half, 1)

    def join_halves(own, other):
        return jnp.where(
            core == 0, jnp.concatenate([own, other], 1), jnp.concatenate([other, own], 1)
        )

    keys, values, queries, cot = (a[0] for a in (key_tokens, value_tokens, query_tokens, cotangent))
    stacked = jnp.concatenate([keys, queries], 0)
    stacked_sibling = swap_cores(stacked)
    cot_sibling = swap_cores(other_half(cot))

    rows = base_weight.shape[0]
    mine = own_half(base_weight)
    weight = lax.all_to_all(
        jnp.broadcast_to(mine[None], (width // rows, rows, half)), DP, 0, 0, tiled=True
    ).reshape(width, half)

    projected_sibling = jnp.dot(stacked_sibling, weight, preferred_element_type=jnp.float32)
    projected = jnp.dot(stacked, weight, preferred_element_type=jnp.float32)
    projected = join_halves(projected, swap_cores(projected_sibling))
    key_proj = projected[None, :slice_len]
    query_proj = projected[None, slice_len:]
    key_wide = key_tokens.astype(jnp.float32)
    value_wide = value_tokens.astype(jnp.float32)
    query_wide = query_tokens.astype(jnp.float32)

    def local_chain(proj, memory):
        memory, lowrank = memory_step(memory, key_wide, value_wide, query_wide, proj)
        return (lowrank, memory)

    memory = factors[None]
    for step in range(seq_count - 1):
        _, passed = local_chain(key_proj, memory)
        moved = lax.ppermute(passed, SEQ, [(step, step + 1)])
        memory = jnp.where(position == step + 1, moved, memory)
    (lowrank, final_memory), pullback = jax.vjp(local_chain, key_proj, memory)
    recalled = (query_proj + lowrank).astype(jnp.bfloat16)
    cot_wide = cotangent.astype(jnp.float32)
    memory_cot = jnp.zeros_like(final_memory)
    for step in reversed(range(seq_count - 1)):
        _, memory_grad = pullback((cot_wide, memory_cot))
        moved = lax.ppermute(memory_grad.astype(jnp.bfloat16), SEQ, [(step + 1, step)])
        memory_cot = jnp.where(position == step, moved.astype(memory_grad.dtype), memory_cot)
    proj_grad, _ = pullback((cot_wide, memory_cot))
    proj_grad = proj_grad[0].astype(jnp.bfloat16)
    proj_sibling = swap_cores(other_half(proj_grad))

    grad_left = jnp.concatenate([stacked, stacked_sibling], 0)
    grad_right = jnp.concatenate([own_half(proj_grad), own_half(cot), proj_sibling, cot_sibling], 0)
    partial = lax.dot_general(
        grad_left, grad_right, (((0,), (0,)), ((), ())), preferred_element_type=jnp.float32
    )
    peak = jnp.max(jnp.abs(partial), axis=1, keepdims=True)
    power = jnp.clip(jnp.ceil(jnp.log2(jnp.maximum(peak, 1e-30))), -100.0, 120.0)
    scaled = (partial * jnp.exp2(-power)).astype(jnp.float16)
    beside = jnp.broadcast_to(power, (width, 128)).astype(jnp.float16)
    sent = jnp.concatenate([scaled, beside], 1)
    got = lax.all_to_all(sent, CHIPS, 0, 0, tiled=True).reshape(64, rows // 2, half + 128)
    factor = jnp.exp2(got[:, :, half : half + 1].astype(jnp.float32))
    share = jnp.sum(got[:, :, :half].astype(jnp.float32) * factor, 0)
    share = join_halves(share, swap_cores(share))
    share_other = lax.ppermute(share, "yl", [(0, 1), (1, 0)])
    base_grad = jnp.where(
        lax.axis_index("yl") == 0,
        jnp.concatenate([share, share_other], 0),
        jnp.concatenate([share_other, share], 0),
    )
    return (recalled, base_grad)


def solution(mesh):
    fine = Mesh(mesh.devices.reshape(4, 4, 2, 2, 2), ("x", "z", "yh", "yl", "c"))
    tokens = P(DP, SEQ, None)
    in_specs = (tokens, tokens, tokens, tokens, P(DP, None), P())
    out_specs = (tokens, P(DP, None))
    return jax.shard_map(
        per_device, mesh=fine, in_specs=in_specs, out_specs=out_specs, check_vma=False
    )
```

time: 757 us -> 342 us (0.45)
  waiting for transfers between devices: 617 us -> 105 us
  blocking collectives: 0 us -> 65.4 us
  local copies, waits for them, and re-layouts: 4.13 us -> 23.3 us
  other arithmetic: 5.57 us -> 23.1 us
  between operations: 14.8 us -> 1.72 us
  starting transfers between devices: 19.4 us -> 30.2 us
    reduce_scatter x1 -> x0, waiting for transfers between devices: 360 us -> none  [per_device(): lax.psum_scatter(lax.dot_general(columns, grad_right, (((0,), (0,)), ((),...]
    all_gather x1 -> x0, waiting for transfers between devices: 107 us -> none  [per_device(): lax.all_gather(base_weight, 'dp', axis=0, tiled=True)]
    all_to_all x0 -> x1, blocking collectives: none -> 65.4 us  [per_device(): lax.all_to_all(sent, CHIPS, 0, 0, tiled=True)]
    ppermute x6 -> x12, waiting for transfers between devices: 110 us -> 55.6 us  [the longest x3 26.3 us: per_device(): moved = lax.ppermute(passed, SEQ, [(step, step + 1)])]
    all_to_all x0 -> x1, waiting for transfers between devices: none -> 49.1 us  [per_device(): lax.all_to_all(jnp.broadcast_to(mine[None], (width // rows, rows, half)),...]
    psum x1 -> x0, waiting for transfers between devices: 39.8 us -> none  [per_device(): base_grad = lax.psum(share, 'seq')]
    all_to_all x0 -> x1, starting transfers between devices: none -> 11.6 us  [per_device(): lax.all_to_all(jnp.broadcast_to(mine[None], (width // rows, rows, half)),...]
    select_n x3 -> x9, other arithmetic: 2.58 us -> 13.5 us  [the longest x3 6.82 us: per_device(): memory = jnp.where(position == step + 1, moved, memory)]
  transfers between devices with their start and end apart: 9 -> 13, of which waited for: 9 -> 8; matrix products, arithmetic and copies ran while one was open for 1% -> 7% of each run, Pallas kernels for 0% -> 0%
where the time goes in v1:
time: 342 us; the launch traced here: 338 us
  waiting for transfers between devices  105 us (31%)
  matrix products  89.7 us (26%)
  blocking collectives  65.4 us (19%)
  starting transfers between devices  30.2 us (9%)
  local copies, waits for them, and re-layouts  23.3 us (7%)
  other arithmetic  23.1 us (7%)
    all_to_all x1, blocking collectives, per_device(): lax.all_to_all(sent, CHIPS, 0, 0, tiled=True)  65.4 us
    all_to_all x1, waiting for transfers between devices, per_device(): lax.all_to_all(jnp.broadcast_to(mine[None], (width // rows, rows, half)),...  49.1 us
    ppermute x3, waiting for transfers between devices, per_device(): moved = lax.ppermute(passed, SEQ, [(step, step + 1)])  26.3 us
    ppermute x3, waiting for transfers between devices, per_device(): lax.ppermute(memory_grad.astype(jnp.bfloat16), SEQ, [(step + 1, step)])  20 us
    dot_general x10, matrix products, memory_step(): jnp.einsum('btr,bdr->btd', key_left, right_factor, precision=highest)  19.2 us
    dot_general x10, matrix products, memory_step(): jnp.einsum('btd,bdr->btr', residue, right_factor, precision=highest)  17 us
    dot_general x9, matrix products, memory_step(): jnp.einsum('btd,btr->bdr', residue, key_left, precision=highest) / GROUP  16.1 us
    all_to_all x1, starting transfers between devices, per_device(): lax.all_to_all(jnp.broadcast_to(mine[None], (width // rows, rows, half)),...  11.6 us
  transfers between devices with their start and end apart: 13, of which 8 were waited for; matrix products, arithmetic and copies ran while one was open for 7% of the time, Pallas kernels for 0%

profile of v1, /device:TPU:1, one launch (start us, length us, event | category | flops | bytes accessed | tf_op | source)
XLA Modules:
  0.0 338.2 jit_solution(411595612129523014)
XLA Ops:
  1.6 2.6 broadcast_in_dim.38
  4.2 11.6 %all-to-all-start = ((bf16[32,64,1024]{2,1,0:T(8,128)(2,1)}), bf16[32,64,1024]{2,1,0:T(8,128)(2,1)}, u32[]{:S(2)}, u32[]{:S(2)}) async-start(bf16[32,64,1024]{2,1,0:T(8,128)(2,1)} %broadcast_in_dim.38), calls=%async_computation | async-start | bytes 8388608 | tf_op jit(solution)/shard_map/all_to_all | solution.py:64
  17.1 3.8 %collective-permute-done = bf16[512,2048]{1,0:T(8,128)(2,1)S(1)} collective-permute-done((bf16[512,2048]{1,0:T(8,128)(2,1)S(1)}, bf16[512,2048]{1,0:T(8,128)(2,1)S(1)}, u32[]{:S(2)}, u32[]{:S(2)}) %collective-permute-start) | collective-permute-done | bytes 2097184 | tf_op jit(solution)/shard_map/ppermute | solution.py:16
  20.9 49.1 %all-to-all-done = bf16[32,64,1024]{2,1,0:T(8,128)(2,1)} async-done(((bf16[32,64,1024]{2,1,0:T(8,128)(2,1)}), bf16[32,64,1024]{2,1,0:T(8,128)(2,1)}, u32[]{:S(2)}, u32[]{:S(2)}) %all-to-all-start) | async-done | bytes 4194336 | tf_op jit(solution)/shard_map/all_to_all | solution.py:64
  70.0 5.9 %fusion.142 = f32[512,1024]{1,0:T(8,128)} fusion(bf16[512,2048]{1,0:T(8,128)(2,1)S(1)} %collective-permute-done, bf16[2048,1024]{1,0:T(8,128)(2,1)} %bitcast.2), kind=kOutput, calls=%fused_computation.220 | convolution fusion | flops 2147483648 | bytes 8388608 | tf_op jit(solution)/shard_map/dot_general | solution.py:68
  75.9 2.9 collective-permute-start.1
  82.7 4.5 %fusion.141 = f32[512,1024]{1,0:T(8,128)S(1)} fusion(bf16[2048,1024]{1,0:T(8,128)(2,1)} %bitcast.2, bf16[256,2048]{1,0:T(8,128)(2,1)S(1)} %bitcast.424, bf16[256,2048]{1,0:T(8,128)(2,1)S(1)} %bitcast.415), kind=kOutput, calls=%fused_computation.219 | convolution fusion | flops 2151677952 | bytes 8388608 | tf_op jit(solution)/shard_map/dot_general | solution.py:69
  87.2 3.1 maximum_select_fusion
  97.9 4.7 %collective-permute-done.2 = f32[1,2,2048,128]{2,3,1,0:T(8,128)} collective-permute-done((f32[1,2,2048,128]{2,3,1,0:T(8,128)S(1)}, f32[1,2,2048,128]{2,3,1,0:T(8,128)}, u32[]{:S(2)}, u32[]{:S(2)}) %collective-permute-start.2) | collective-permute-done | bytes 2097184 | tf_op jit(solution)/shard_map/ppermute | solution.py:84
  102.6 2.7 broadcast_select_fusion
  113.6 2.7 collective-permute-start.3
  116.3 21.6 %collective-permute-done.3 = f32[1,2,2048,128]{2,3,1,0:T(8,128)} collective-permute-done((f32[1,2,2048,128]{2,3,1,0:T(8,128)S(1)}, f32[1,2,2048,128]{2,3,1,0:T(8,128)}, u32[]{:S(2)}, u32[]{:S(2)}) %collective-permute-start.3) | collective-permute-done | bytes 2097184 | tf_op jit(solution)/shard_map/ppermute | solution.py:84
  148.3 2.4 collective-permute-start.4
  166.9 2.4 fusion.49
  179.6 2.3 convolution_bitcast_fusion.13
  187.1 20.0 %collective-permute-done.6 = bf16[1,2,2048,128]{2,3,1,0:T(8,128)(2,1)S(1)} collective-permute-done((bf16[1,2,2048,128]{2,3,1,0:T(8,128)(2,1)S(1)}, bf16[1,2,2048,128]{2,3,1,0:T(8,128)(2,1)S(1)}, u32[]{:S(2)}, u32[]{:S(2)}) %collective-permute-start.6) | collective-permute-done | bytes 1048608 | tf_op jit(solution)/shard_map/ppermute | solution.py:92
  214.7 2.3 convolution_bitcast_fusion.11
  223.7 2.3 dynamic-slice_bitcast_fusion.2
  235.4 5.9 %abs_reduce_fusion = (f32[2048]{0:T(1024)S(1)}, f32[2048,1024]{0,1:T(8,128)S(1)}) fusion(bf16[256,1024]{1,0:T(8,128)(2,1)} %collective-permute-done.9, bf16[256,1024]{1,0:T(8,128)(2,1)S(1)} %collective-permute-done.8, bf16[256,1024]{1,0:T(8,128)(2,1)S(1)} %copy-done.21, bf16[256,1024]{1,0:T(8,128)(2,1)S(1)} %get-tuple-element.4, ...), kind=kOutput, calls=%fused_computation.2 | convolution fusion | flops 4320131072 | bytes 14688256 | tf_op jit(solution)/shard_map/dot_general | solution.py:100
  242.6 3.6 %pad_maximum_fusion = f16[2048,1152]{0,1:T(8,128)(2,1)} fusion(f16[2048,128]{0,1:T(8,128)(2,1)S(1)} %broadcast_in_dim.47, f16[2048,1024]{0,1:T(8,128)(2,1)S(1)} %multiply_convert_fusion), kind=kLoop, calls=%fused_computation.3 | loop fusion | flops 2359296 | bytes 9437184 | tf_op jit(solution)/shard_map/concatenate | solution.py:107
  246.2 7.1 %copy.91 = f16[2048,1152]{1,0:T(8,128)(2,1)} copy(f16[2048,1152]{0,1:T(8,128)(2,1)} %pad_maximum_fusion) | data formatting | bytes 9437184 | tf_op jit(solution)/shard_map/concatenate | solution.py:107
  253.3 65.4 %all_to_all.14 = f16[64,32,1152]{2,1,0:T(8,128)(2,1)S(1)} all-to-all(f16[64,32,1152]{2,1,0:T(8,128)(2,1)} %bitcast.422), channel_id=1, replica_groups=mesh['x'=4,'z'=4,'yh'=2,'yl'=2,'c'=2] {'x','z','yh','yl'}, dimensions={0} | all-to-all | bytes 9437184 | tf_op jit(solution)/shard_map/all_to_all | solution.py:108
  321.9 2.7 multiply_reduce_fusion
  330.7 4.5 %fusion.54 = bf16[1,256,2048]{2,1,0:T(8,128)(2,1)} fusion(f32[512,2048]{1,0:T(8,128)} %copy-done.3, f32[128,256]{1,0:T(8,128)S(1)} %fusion.91, f32[1,2,2048,128]{2,3,1,0:T(8,128)S(1)} %broadcast_select_fusion.2), kind=kOutput, calls=%fused_computation.108 | convolution fusion | flops 806354944 | bytes 4325376 | tf_op jit(solution)/shard_map/jvp(btr,bdr->btd)/dot_general | solution.py:24
  (135 shorter events, 100.5 us)
Async XLA Ops:
  4.2 11.6 %copy-start.2 = (bf16[1,256,2048]{2,1,0:T(8,128)(2,1)S(1)}, bf16[1,256,2048]{2,1,0:T(8,128)(2,1)}, u32[]{:S(2)}) copy-start(bf16[1,256,2048]{2,1,0:T(8,128)(2,1)} %param.6) | copy-start | bytes 3145732
  4.2 11.6 %copy-start.17 = (bf16[1,256,2048]{2,1,0:T(8,128)(2,1)S(1)}, bf16[1,256,2048]{2,1,0:T(8,128)(2,1)}, u32[]{:S(2)}) copy-start(bf16[1,256,2048]{2,1,0:T(8,128)(2,1)} %param.8) | copy-start | bytes 3145732
  4.2 65.8 %all-to-all-start = ((bf16[32,64,1024]{2,1,0:T(8,128)(2,1)}), bf16[32,64,1024]{2,1,0:T(8,128)(2,1)}, u32[]{:S(2)}, u32[]{:S(2)}) async-start(bf16[32,64,1024]{2,1,0:T(8,128)(2,1)} %broadcast_in_dim.38), calls=%async_computation | async-start | bytes 8388608 | tf_op jit(solution)/shard_map/all_to_all | solution.py:64
  16.1 4.8 %collective-permute-start = (bf16[512,2048]{1,0:T(8,128)(2,1)S(1)}, bf16[512,2048]{1,0:T(8,128)(2,1)S(1)}, u32[]{:S(2)}, u32[]{:S(2)}) collective-permute-start(bf16[512,2048]{1,0:T(8,128)(2,1)S(1)} %pad_maximum_fusion.1), channel_id=1, source_target_pairs={{0,1},{1,0},{2,3},{3,2},{4,5},{5,4},{6,7},{7,6},{8,9},{9,8},{10,11... | collective-permute-start | bytes 6291464 | tf_op jit(solution)/shard_map/ppermute | solution.py:16
  20.9 55.0 %copy-start.22 = (bf16[512,2048]{1,0:T(8,128)(2,1)}, bf16[512,2048]{1,0:T(8,128)(2,1)S(1)}, u32[]{:S(2)}) copy-start(bf16[512,2048]{1,0:T(8,128)(2,1)S(1)} %collective-permute-done) | copy-start | bytes 6291460
  75.9 11.3 %collective-permute-start.1 = (f32[512,1024]{1,0:T(8,128)}, f32[512,1024]{1,0:T(8,128)}, u32[]{:S(2)}, u32[]{:S(2)}) collective-permute-start(f32[512,1024]{1,0:T(8,128)} %fusion.142), channel_id=1, source_target_pairs={{0,1},{1,0},{2,3},{3,2},{4,5},{5,4},{6,7},{7,6},{8,9},{9,8},{10,11... | collective-permute-start | bytes 6291464 | tf_op jit(solution)/shard_map/ppermute | solution.py:16
  80.7 14.9 %copy-start.10 = (f32[2,2048,128]{1,2,0:T(8,128)}, f32[2,2048,128]{1,2,0:T(8,128)S(1)}, u32[]{:S(2)}) copy-start(f32[2,2048,128]{1,2,0:T(8,128)S(1)} %copy.79) | copy-start | bytes 6291460
  96.4 6.2 %collective-permute-start.2 = (f32[1,2,2048,128]{2,3,1,0:T(8,128)S(1)}, f32[1,2,2048,128]{2,3,1,0:T(8,128)}, u32[]{:S(2)}, u32[]{:S(2)}) collective-permute-start(f32[1,2,2048,128]{2,3,1,0:T(8,128)S(1)} %pad_maximum_fusion.2), channel_id=1, source_target_pairs={{0,1},{4,5},{8,9},{12,13},{16,17},{20,21},{24,25},{28,29},{32,33},... | collective-permute-start | bytes 6291464 | tf_op jit(solution)/shard_map/ppermute | solution.py:84
  102.6 3.9 %copy-start.4 = (f32[512,2048]{1,0:T(8,128)S(1)}, f32[512,2048]{1,0:T(8,128)}, u32[]{:S(2)}) copy-start(f32[512,2048]{1,0:T(8,128)} %copy-done.3) | copy-start | bytes 12582916
  105.3 7.4 %copy-start.8 = (f32[1,2,2048,128]{2,3,1,0:T(8,128)}, f32[1,2,2048,128]{2,3,1,0:T(8,128)S(1)}, u32[]{:S(2)}) copy-start(f32[1,2,2048,128]{2,3,1,0:T(8,128)S(1)} %broadcast_select_fusion) | copy-start | bytes 6291460
  113.6 24.3 %collective-permute-start.3 = (f32[1,2,2048,128]{2,3,1,0:T(8,128)S(1)}, f32[1,2,2048,128]{2,3,1,0:T(8,128)}, u32[]{:S(2)}, u32[]{:S(2)}) collective-permute-start(f32[1,2,2048,128]{2,3,1,0:T(8,128)S(1)} %pad_maximum_fusion.3), channel_id=1, source_target_pairs={{1,2},{5,6},{9,10},{13,14},{17,18},{21,22},{25,26},{29,30},{33,34}... | collective-permute-start | bytes 6291464 | tf_op jit(solution)/shard_map/ppermute | solution.py:84
  137.9 3.3 copy-start.5
  140.0 7.4 %copy-start.7 = (f32[1,2,2048,128]{2,3,1,0:T(8,128)}, f32[1,2,2048,128]{2,3,1,0:T(8,128)S(1)}, u32[]{:S(2)}) copy-start(f32[1,2,2048,128]{2,3,1,0:T(8,128)S(1)} %broadcast_select_fusion.1) | copy-start | bytes 6291460
  148.3 3.6 %collective-permute-start.4 = (f32[1,2,2048,128]{2,3,1,0:T(8,128)S(1)}, f32[1,2,2048,128]{2,3,1,0:T(8,128)}, u32[]{:S(2)}, u32[]{:S(2)}) collective-permute-start(f32[1,2,2048,128]{2,3,1,0:T(8,128)S(1)} %pad_maximum_fusion.4), channel_id=1, source_target_pairs={{2,3},{6,7},{10,11},{14,15},{18,19},{22,23},{26,27},{30,31},{34,35... | collective-permute-start | bytes 6291464 | tf_op jit(solution)/shard_map/ppermute | solution.py:84
  171.4 0.7 collective-permute-start.5
  185.4 21.7 %collective-permute-start.6 = (bf16[1,2,2048,128]{2,3,1,0:T(8,128)(2,1)S(1)}, bf16[1,2,2048,128]{2,3,1,0:T(8,128)(2,1)S(1)}, u32[]{:S(2)}, u32[]{:S(2)}) collective-permute-start(bf16[1,2,2048,128]{2,3,1,0:T(8,128)(2,1)S(1)} %add_convert_fusion.1), channel_id=1, source_target_pairs={{2,1},{6,5},{10,9},{14,13},{18,17},{22,21},{26,25},{30,29},{34,33}... | collective-permute-start | bytes 3145736 | tf_op jit(solution)/shard_map/ppermute | solution.py:92
  207.4 12.2 %copy-start.9 = (f32[1,2,2048,128]{2,3,1,0:T(8,128)}, f32[1,2,2048,128]{2,3,1,0:T(8,128)S(1)}, u32[]{:S(2)}) copy-start(f32[1,2,2048,128]{2,3,1,0:T(8,128)S(1)} %convert_select_fusion.1) | copy-start | bytes 6291460
  221.5 4.5 %collective-permute-start.7 = (bf16[1,2,2048,128]{2,3,1,0:T(8,128)(2,1)}, bf16[1,2,2048,128]{2,3,1,0:T(8,128)(2,1)}, u32[]{:S(2)}, u32[]{:S(2)}) collective-permute-start(bf16[1,2,2048,128]{2,3,1,0:T(8,128)(2,1)} %add_convert_fusion), channel_id=1, source_target_pairs={{1,0},{5,4},{9,8},{13,12},{17,16},{21,20},{25,24},{29,28},{33,32},... | collective-permute-start | bytes 3145736 | tf_op jit(solution)/shard_map/ppermute | solution.py:92
  226.0 7.5 %collective-permute-start.9 = (bf16[256,1024]{1,0:T(8,128)(2,1)}, bf16[256,1024]{1,0:T(8,128)(2,1)}, u32[]{:S(2)}, u32[]{:S(2)}) collective-permute-start(bf16[256,1024]{1,0:T(8,128)(2,1)} %get-tuple-element.7), channel_id=1, source_target_pairs={{0,1},{1,0},{2,3},{3,2},{4,5},{5,4},{6,7},{7,6},{8,9},{9,8},{10,11... | collective-permute-start | bytes 1572872 | tf_op jit(solution)/shard_map/ppermute | solution.py:16
  231.1 4.3 %copy-start.23 = (bf16[512,2048]{1,0:T(8,128)(2,1)S(1)}, bf16[512,2048]{1,0:T(8,128)(2,1)}, u32[]{:S(2)}) copy-start(bf16[512,2048]{1,0:T(8,128)(2,1)} %copy-done.22) | copy-start | bytes 6291460
  233.2 2.2 collective-permute-start.8
  325.7 3.7 %collective-permute-start.10 = (f32[32,1024]{0,1:T(8,128)}, f32[32,1024]{0,1:T(8,128)S(1)}, u32[]{:S(2)}, u32[]{:S(2)}) collective-permute-start(f32[32,1024]{0,1:T(8,128)} %copy.110), channel_id=1, source_target_pairs={{0,1},{1,0},{2,3},{3,2},{4,5},{5,4},{6,7},{7,6},{8,9},{9,8},{10,11... | collective-permute-start | bytes 393224 | tf_op jit(solution)/shard_map/ppermute | solution.py:16
  329.6 7.6 %collective-permute-start.11 = (f32[32,2048]{1,0:T(8,128)S(1)}, f32[32,2048]{1,0:T(8,128)S(1)}, u32[]{:S(2)}, u32[]{:S(2)}) collective-permute-start(f32[32,2048]{1,0:T(8,128)S(1)} %maximum_select_fusion.2), channel_id=1, source_target_pairs={{0,2},{2,0},{1,3},{3,1},{4,6},{6,4},{5,7},{7,5},{8,10},{10,8},{9,1... | collective-permute-start | bytes 786440 | tf_op jit(solution)/shard_map/ppermute | solution.py:112
  330.7 7.3 %copy-start.1 = (bf16[64,2048]{1,0:T(8,128)(2,1)S(1)}, bf16[64,2048]{1,0:T(8,128)(2,1)}, u32[]{:S(2)}) copy-start(bf16[64,2048]{1,0:T(8,128)(2,1)} %param.10) | copy-start | bytes 786436
  (13 other events, 28.2 us)
